TPU v7x, 256 devices: a whole 4x4x8 slice. The times are simulated.
256 devices in a mesh: ctx: 16 (over x, y), ksplit: 16 (over z, core).
Axes of the slice: x: 4, y: 4, z: 8, core: 2. Of those that a mesh axis runs over, the one named last changes fastest.
Arguments:
- queries: bfloat16 [8192, 32, 128], P('ctx'), may hold values from -5 to 5
- stretch_kv: bfloat16 [8192, 8, 256], P('ctx'), may hold values from -5 to 5
- prefix_kv: bfloat16 [1024, 64, 8, 256], P(('ctx', 'ksplit')), may hold values from -5 to 5
- vertical: int32 [8, 64], replicated, may hold values from 0 to 1023, as said below
- slash_offsets: int32 [32, 32], replicated, may hold values from 0 to 39, as said below
- block_home: int32 [1024], replicated, may hold values from 0 to 1023, as said below
Outputs:
- attention: bfloat16 [8192, 4096], P('ctx', 'ksplit')
Inputs may be any that keep to these rules, and one draw needn't show every extreme that they name: `vertical`: each row names 64 different prefix blocks; entry j names a block whose slot, divided by 4, is a device number d of ctx+ksplit with d mod 16 = j mod 16. `slash_offsets`: each row holds 32 different offsets, 0 among them. `block_home`: A permutation.
All inputs are finite; a program needn't handle non-finite values.
Results may differ from a plain program's by a relative error of at most 0.0055.
Values may be sent and summed in bfloat16 or wider, within the bound.
A program may use at most 192 MiB of HBM per device.

v0:
```python
import math

import jax
import jax.numpy as jnp
from jax import lax
from jax.sharding import PartitionSpec as P

BLOCK = 64
SPAN = 40


def passed_along(block, axis, distance):
    devices = range(lax.axis_size(axis))
    route = [(i - distance, i) for i in devices if i - distance in devices]
    return lax.ppermute(block, axis, route)


def combine_stack(received):
    stack_lse, stack_out = received
    lse_top = jnp.max(stack_lse, 0)
    lse_all = lse_top + jnp.log(jnp.sum(jnp.exp(stack_lse - lse_top), 0))
    weights = jnp.exp(stack_lse - lse_all)
    merged = jnp.sum(weights[..., None] * stack_out, 0)
    return merged.reshape(merged.shape[0], -1).astype(jnp.bfloat16)


def slash_terms(slash_scores, slash_key_value, own_top, block_count, head_dim):
    own_heads = slash_scores.shape[0]
    row_count = slash_scores.shape[1]
    slash_weight_matrix = jnp.exp(slash_scores - own_top[..., None])
    slash_total = jnp.sum(slash_weight_matrix, 2)
    slash_probs = slash_weight_matrix.astype(jnp.bfloat16).reshape(
        own_heads, block_count, BLOCK, -1
    )
    slash_values = slash_key_value[..., head_dim:].reshape(own_heads, block_count, -1, head_dim)
    slash_accumulator = jnp.einsum(
        "hqtm,hqmd->hqtd", slash_probs, slash_values, preferred_element_type=jnp.float32
    )
    return (slash_total, slash_accumulator.reshape(own_heads, row_count, head_dim))


def on_device(queries, stretch_kv, prefix_kv, vertical, slash_offsets, block_home):
    row_count, head_count, head_dim = queries.shape
    kv_count = stretch_kv.shape[1]
    group_size = head_count // kv_count
    partners = lax.axis_size("ksplit")
    partner = lax.axis_index("ksplit")
    owner_index = lax.axis_index("ctx")
    block_count = row_count // BLOCK
    own_heads = head_count // partners
    first_head = partner * own_heads
    kv_group = first_head // group_size
    score_scale = 1.0 / math.sqrt(head_dim)
    local_blocks = prefix_kv.shape[0]
    shares = vertical.shape[1] // partners
    by_partner = vertical.reshape(kv_count, shares, partners)
    entries = jnp.sum(jnp.where(jnp.arange(partners) == partner, by_partner, 0), 2)
    block_ids = jnp.arange(block_home.shape[0])
    slot_ids = jnp.sum(jnp.where(entries[..., None] == block_ids, block_home, 0), 2)
    held_here = slot_ids // local_blocks == owner_index * partners + partner
    selector = ((slot_ids % local_blocks)[..., None] == jnp.arange(local_blocks)) & held_here[
        ..., None
    ]
    pieces = jnp.einsum(
        "gvr,rtgk->gvtk",
        selector.astype(jnp.bfloat16),
        prefix_kv,
        preferred_element_type=jnp.float32,
    )
    gathered = lax.psum(pieces.astype(jnp.bfloat16), "ctx")
    hop_count = (SPAN - 1) // block_count + 1
    layers = [stretch_kv]
    for distance in range(1, hop_count + 1):
        layers.append(passed_along(stretch_kv, "ctx", distance))
    window = jnp.concatenate(layers[::-1], 0)
    window = lax.dynamic_index_in_dim(window, kv_group, 1, keepdims=False)
    window_blocks = window.reshape(-1, BLOCK, 2 * head_dim)
    offsets = lax.dynamic_slice_in_dim(slash_offsets, first_head, own_heads, 0)
    local_index = jnp.arange(block_count)
    block_index = hop_count * block_count + local_index[None, :, None] - offsets[:, None, :]
    slash_key_value = window_blocks[block_index]
    reachable = (owner_index * block_count + local_index)[None, :, None] - offsets[:, None, :] >= 0
    own_rows = lax.dynamic_slice_in_dim(queries, first_head, own_heads, 1)
    own_queries = own_rows.reshape(block_count, BLOCK, own_heads, head_dim)
    slash_scores = (
        jnp.einsum(
            "qthd,hqnsd->hqtns",
            own_queries,
            slash_key_value[..., :head_dim],
            preferred_element_type=jnp.float32,
        )
        * score_scale
    )
    position = jnp.arange(BLOCK)
    causal = position[None, :] <= position[:, None]
    allowed = reachable[:, :, None, :, None] & (
        (offsets != 0)[:, None, None, :, None] | causal[None, None, :, None, :]
    )
    slash_scores = jnp.where(allowed, slash_scores, -jnp.inf).reshape(own_heads, row_count, -1)
    slash_top = jnp.max(slash_scores, 2)
    vertical_kv = gathered.reshape(kv_count, shares * BLOCK, 2 * head_dim)
    grouped_heads = queries.reshape(row_count, kv_count, group_size, head_dim)
    vertical_scores = (
        jnp.einsum(
            "rghd,gkd->grhk",
            grouped_heads,
            vertical_kv[..., :head_dim],
            preferred_element_type=jnp.float32,
        )
        * score_scale
    )
    vertical_top = jnp.max(vertical_scores, 3).transpose(1, 0, 2).reshape(row_count, head_count)
    empty_top = jnp.full((row_count, head_count), -jnp.inf, jnp.float32)
    slash_full = lax.dynamic_update_slice_in_dim(empty_top, slash_top.T, first_head, 1)
    joint_top = jnp.maximum(vertical_top, slash_full)
    top_grouped = joint_top.reshape(row_count, kv_count, group_size).transpose(1, 0, 2)
    vertical_weights = jnp.exp(vertical_scores - top_grouped[..., None])
    vertical_total = jnp.sum(vertical_weights, 3).transpose(1, 0, 2).reshape(row_count, head_count)
    vertical_acc = jnp.einsum(
        "grhk,gkd->rghd",
        vertical_weights.astype(jnp.bfloat16),
        vertical_kv[..., head_dim:],
        preferred_element_type=jnp.float32,
    )
    vertical_acc = vertical_acc.reshape(row_count, head_count, head_dim)
    own_top = lax.dynamic_slice_in_dim(joint_top, first_head, own_heads, 1).T
    slash_total, slash_accumulator = slash_terms(
        slash_scores, slash_key_value, own_top, block_count, head_dim
    )
    totals = vertical_total + lax.dynamic_update_slice_in_dim(
        jnp.zeros_like(vertical_total), slash_total.T, first_head, 1
    )
    accumulated = vertical_acc + lax.dynamic_update_slice_in_dim(
        jnp.zeros_like(vertical_acc), slash_accumulator.transpose(1, 0, 2), first_head, 1
    )
    partial_lse = joint_top + jnp.log(totals)
    partial_out = lax.optimization_barrier(
        (accumulated / totals[..., None]).astype(jnp.bfloat16)
    ).astype(jnp.float32)
    return combine_stack(
        (
            lax.all_to_all(partial_lse[None], "ksplit", split_axis=2, concat_axis=0, tiled=True),
            lax.all_to_all(partial_out[None], "ksplit", split_axis=2, concat_axis=0, tiled=True),
        )
    )


def solution(mesh):
    return jax.shard_map(
        on_device,
        mesh=mesh,
        in_specs=(
            P("ctx", None, None),
            P("ctx", None, None),
            P(("ctx", "ksplit"), None, None, None),
            P(),
            P(),
            P(),
        ),
        out_specs=P("ctx", "ksplit"),
        check_vma=False,
    )
```

profile of v0, /device:TPU:4, one launch (start us, length us, event | category | flops | bytes accessed | tf_op | source)
XLA Modules:
  0.0 650.7 jit_solution(10210361202474992357)
XLA Ops:
  6.5 3.5 copy.67
  10.0 3.5 collective-permute-start.4
  13.5 4.8 collective-permute-start.3
  18.3 3.9 collective-permute-start.2
  22.2 1.9 collective-permute-start.1
  24.1 1.9 collective-permute-start
  26.1 0.8 reshape.141
  26.8 0.2 select_reduce_fusion.1
  27.1 0.1 copy.60
  27.1 0.9 select_reduce_fusion
  28.1 0.1 copy.62
  28.2 0.1 copy.61
  28.3 1.5 convolution_convert_fusion
  29.7 1.2 copy.64
  31.0 0.7 broadcast_compare_fusion.1
  31.7 1.5 constant_dynamic-slice_fusion.1
  33.3 0.1 reshape.158
  33.5 0.3 broadcast_or_fusion
  33.8 293.6 %all-reduce.2.cloned.1.call-done = bf16[8,256,256]{2,1,0:T(8,128)(2,1)} async-done(((bf16[8,256,256]{2,1,0:T(8,128)(2,1)}), bf16[8,256,256]{2,1,0:T(8,128)(2,1)}) %all-reduce.2.cloned.1.call-update) | async-done | bytes 1048592 | tf_op jit(solution)/shard_map/psum | solution.py:70
  327.4 13.4 %bitcast_reduce_fusion = (f32[8,512,4]{1,2,0:T(4,128)S(1)}, f32[8,256,512,4]{2,1,3,0:T(8,128)}) fusion(bf16[512,8,4,128]{3,2,1,0:T(4,128)(2,1)} %bitcast.98, bf16[8,256,256]{2,1,0:T(8,128)(2,1)} %all-reduce.2.cloned.1.call-done), kind=kOutput, calls=%fused_computation.2 | convolution fusion | flops 1082114048 | bytes 21561344 | tf_op jit(solution)/shard_map/rghd,gkd->grhk/dot_general | solution.py:104
  340.9 1.7 constant_dynamic-update-slice_fusion.5
  342.6 1.9 constant_dynamic-update-slice_fusion.4
  344.5 1.7 constant_dynamic-update-slice_fusion.3
  346.3 1.7 constant_dynamic-update-slice_fusion.2
  348.1 0.1 constant_dynamic-update-slice_fusion.1
  348.2 0.4 constant_dynamic-update-slice_fusion
  348.6 0.1 constant_dynamic-slice_fusion
  348.8 14.1 %gather_fusion = bf16[512,64,256]{2,1,0:T(8,128)(2,1)} fusion(bf16[48,64,256]{2,1,0:T(8,128)(2,1)S(1)} %bitcast.92, s32[1024]{0:T(1024)S(1)} %pad_clamp_fusion), kind=kCustom, calls=%fused_computation | custom fusion | bytes 33556480 | tf_op jit(solution)/shard_map/gather | solution.py:81
  362.8 9.4 %slice.21 = bf16[2,8,32,64,128]{4,3,2,1,0:T(8,128)(2,1)} slice(bf16[2,8,32,64,256]{4,3,2,1,0:T(8,128)(2,1)} %bitcast.94), slice={[0:2], [0:8], [0:32], [0:64], [128:256]} | slice | bytes 16777216 | tf_op jit(solution)/shard_map/slice | solution.py:35
  372.2 9.8 %fusion.29 = (f32[2,8,64]{2,1,0:T(8,128)S(1)}, f32[2,8,64,32,64]{2,4,3,1,0:T(8,128)}) fusion(bf16[8,64,2,128,1]{3,1,4,0,2:T(8,128)(2,1)S(1)} %bitcast.109, bf16[2,8,32,64,256]{4,3,2,1,0:T(8,128)(2,1)} %bitcast.95, pred[2,64,32,64]{1,3,2,0:T(8,128)(4,1)S(1)} %broadcast_or_fusion, pred[2,8,32]{2,1,0:T(8,128)(4,1)S(1)} %subtract_compare_fusion), kind=kOutput, calls=%fused_computation.74 | convolution fusion | flops 545258496 | bytes 17306112 | tf_op jit(solution)/shard_map/qthd,hqnsd->hqtns/dot_general | solution.py:86
  382.2 12.7 %copy.75 = f32[2,8,64,2048]{3,2,1,0:T(8,128)} copy(f32[2,8,64,2048]{2,3,1,0:T(8,128)} %bitcast.93) | data formatting | bytes 16777216 | tf_op jit(solution)/shard_map/reshape | solution.py:99
  394.9 0.1 sub.101
  394.9 8.5 %exponential_reduce_fusion = f32[2,8,64]{2,1,0:T(8,128)S(1)} fusion(f32[2,8,64,32,64]{2,4,3,1,0:T(8,128)} %get-tuple-element.10, f32[2,8,64]{2,1,0:T(8,128)S(1)} %sub.101), kind=kLoop, calls=%fused_computation.4 | loop fusion | flops 4193280 | bytes 8396800 | tf_op jit(solution)/shard_map/reduce_sum | solution.py:31
  403.4 0.1 reduce_sum.60
  403.5 7.6 %fusion.11 = f32[2,8,64,128]{3,2,1,0:T(8,128)S(1)} fusion(bf16[2,8,2048,128]{3,2,1,0:T(8,128)(2,1)} %bitcast.97, f32[2,8,64,2048]{3,2,1,0:T(8,128)} %copy.75, f32[2,8,64]{2,1,0:T(8,128)S(1)} %sub.101), kind=kOutput, calls=%fused_computation.16 | convolution fusion | flops 541065216 | bytes 17305600 | tf_op jit(solution)/shard_map/hqtm,hqmd->hqtd/dot_general | solution.py:36
  411.1 0.2 copy.76
  411.3 8.8 %fusion.2 = f32[8,512,4]{1,2,0:T(4,128)S(1)} fusion(f32[8,256,512,4]{2,1,3,0:T(8,128)} %get-tuple-element.8, f32[8,512,4]{1,2,0:T(4,128)S(1)} %bitcast.105), kind=kLoop, calls=%fused_computation.7 | loop fusion | flops 12566528 | bytes 16908288 | tf_op jit(solution)/shard_map/reduce_sum | solution.py:118
  420.2 7.4 %fusion.3 = f32[8,128,512,4]{2,1,3,0:T(8,128)S(1)} fusion(f32[8,256,512,4]{2,1,3,0:T(8,128)} %get-tuple-element.8, f32[8,512,4]{1,2,0:T(4,128)S(1)} %bitcast.106, bf16[8,256,256]{2,1,0:T(8,128)(2,1)S(1)} %copy-done.3), kind=kOutput, calls=%fused_computation.8 | convolution fusion | flops 1086324736 | bytes 25755648 | tf_op jit(solution)/shard_map/grhk,gkd->rghd/dot_general | solution.py:119
  427.7 0.1 fusion.16
  427.8 3.3 divide_convert_fusion
  431.1 0.7 broadcast_in_dim.35
  431.8 8.6 %all-to-all-start = ((f32[1,512,32]{1,0,2:T(1,128)}), f32[1,512,32]{1,0,2:T(1,128)S(1)}, u32[]{:S(2)}, u32[]{:S(2)}) async-start(f32[1,512,32]{1,0,2:T(1,128)} %broadcast_in_dim.35), calls=%async_computation | async-start | bytes 131072 | tf_op jit(solution)/shard_map/all_to_all | solution.py:142
  440.4 6.6 %bitcast_convert_fusion = f32[1,512,32,128]{1,3,0,2:T(8,128)} fusion(bf16[512,32,128]{0,2,1:T(8,128)(2,1)} %divide_convert_fusion), kind=kLoop, calls=%fused_computation.17 | loop fusion | flops 2097152 | bytes 12582912 | tf_op jit(solution)/shard_map/broadcast_in_dim | solution.py:143
  447.0 1.3 all-to-all-done
  448.3 6.0 all-to-all-start.1
  454.5 184.0 %all-to-all-done.1 = f32[1,512,32,128]{1,3,0,2:T(8,128)} async-done(((f32[1,512,32,128]{1,3,0,2:T(8,128)}), f32[1,512,32,128]{1,3,0,2:T(8,128)}, u32[]{:S(2)}, u32[]{:S(2)}) %all-to-all-start.1) | async-done | bytes 8388640 | tf_op jit(solution)/shard_map/all_to_all | solution.py:143
  638.5 4.5 multiply_reduce_fusion
  643.0 0.8 copy.77
  (39 shorter events, 0.7 us)
Async XLA Ops:
  6.5 21.7 %copy-start = (bf16[4,64,8,256]{3,2,1,0:T(8,128)(2,1)S(1)}, bf16[4,64,8,256]{3,2,1,0:T(8,128)(2,1)}, u32[]{:S(2)}) copy-start(bf16[4,64,8,256]{3,2,1,0:T(8,128)(2,1)} %param.8) | copy-start | bytes 3145732
  6.5 320.9 %all-reduce.2.cloned.1.call-start = ((), (), s32[]{:S(2)}) async-start(), calls=%async_computation.2 | async-start | bytes 2097152 | tf_op jit(solution)/shard_map/psum | solution.py:70
  10.0 338.1 %collective-permute-start.4 = (bf16[512,8,256]{2,0,1:T(8,128)(2,1)}, bf16[512,8,256]{2,0,1:T(8,128)(2,1)S(1)}, u32[]{:S(2)}, u32[]{:S(2)}) collective-permute-start(bf16[512,8,256]{2,0,1:T(8,128)(2,1)} %copy.67), channel_id=1, source_target_pairs={{0,16},{16,32},{32,48},{48,64},{64,80},{80,96},{96,112},{112,128},... | collective-permute-start | bytes 6291464 | tf_op jit(solution)/shard_map/ppermute | solution.py:15
  13.5 332.8 %collective-permute-start.3 = (bf16[512,8,256]{2,0,1:T(8,128)(2,1)}, bf16[512,8,256]{2,0,1:T(8,128)(2,1)}, u32[]{:S(2)}, u32[]{:S(2)}) collective-permute-start(bf16[512,8,256]{2,0,1:T(8,128)(2,1)} %copy.67), channel_id=1, source_target_pairs={{0,32},{16,48},{32,64},{48,80},{64,96},{80,112},{96,128},{112,144}... | collective-permute-start | bytes 6291464 | tf_op jit(solution)/shard_map/ppermute | solution.py:15
  18.3 326.2 %collective-permute-start.2 = (bf16[512,8,256]{2,0,1:T(8,128)(2,1)}, bf16[512,8,256]{2,0,1:T(8,128)(2,1)}, u32[]{:S(2)}, u32[]{:S(2)}) collective-permute-start(bf16[512,8,256]{2,0,1:T(8,128)(2,1)} %copy.67), channel_id=1, source_target_pairs={{0,48},{16,64},{32,80},{48,96},{64,112},{80,128},{96,144},{112,160... | collective-permute-start | bytes 6291464 | tf_op jit(solution)/shard_map/ppermute | solution.py:15
  22.2 320.4 %collective-permute-start.1 = (bf16[512,8,256]{2,0,1:T(8,128)(2,1)}, bf16[512,8,256]{2,0,1:T(8,128)(2,1)}, u32[]{:S(2)}, u32[]{:S(2)}) collective-permute-start(bf16[512,8,256]{2,0,1:T(8,128)(2,1)} %copy.67), channel_id=1, source_target_pairs={{0,64},{16,80},{32,96},{48,112},{64,128},{80,144},{96,160},{112,17... | collective-permute-start | bytes 6291464 | tf_op jit(solution)/shard_map/ppermute | solution.py:15
  24.1 316.7 %collective-permute-start = (bf16[512,8,256]{2,0,1:T(8,128)(2,1)}, bf16[512,8,256]{2,0,1:T(8,128)(2,1)}, u32[]{:S(2)}, u32[]{:S(2)}) collective-permute-start(bf16[512,8,256]{2,0,1:T(8,128)(2,1)} %copy.67), channel_id=1, source_target_pairs={{0,80},{16,96},{32,112},{48,128},{64,144},{80,160},{96,176},{112,1... | collective-permute-start | bytes 6291464 | tf_op jit(solution)/shard_map/ppermute | solution.py:15
  342.6 5.6 copy-start.2
  411.3 8.9 %copy-start.3 = (bf16[8,256,256]{2,1,0:T(8,128)(2,1)S(1)}, bf16[8,256,256]{2,1,0:T(8,128)(2,1)}, u32[]{:S(2)}) copy-start(bf16[8,256,256]{2,1,0:T(8,128)(2,1)} %all-reduce.2.cloned.1.call-done) | copy-start | bytes 3145732
  431.8 16.5 %all-to-all-start = ((f32[1,512,32]{1,0,2:T(1,128)}), f32[1,512,32]{1,0,2:T(1,128)S(1)}, u32[]{:S(2)}, u32[]{:S(2)}) async-start(f32[1,512,32]{1,0,2:T(1,128)} %broadcast_in_dim.35), calls=%async_computation | async-start | bytes 131072 | tf_op jit(solution)/shard_map/all_to_all | solution.py:142
  448.3 190.2 %all-to-all-start.1 = ((f32[1,512,32,128]{1,3,0,2:T(8,128)}), f32[1,512,32,128]{1,3,0,2:T(8,128)}, u32[]{:S(2)}, u32[]{:S(2)}) async-start(f32[1,512,32,128]{1,3,0,2:T(8,128)} %bitcast_convert_fusion), calls=%async_computation.1 | async-start | bytes 16777216 | tf_op jit(solution)/shard_map/all_to_all | solution.py:143
  454.2 189.6 %copy-start.1 = (bf16[4,64,8,256]{3,2,1,0:T(8,128)(2,1)S(1)}, bf16[4,64,8,256]{3,2,1,0:T(8,128)(2,1)}, u32[]{:S(2)}) copy-start(bf16[4,64,8,256]{3,2,1,0:T(8,128)(2,1)} %param.8) | copy-start | bytes 3145732
Sparse Core Ops, SparseCore 0:
  31.1 296.2 all-reduce.1
where the time goes:
time: 652 us; the launch traced here: 651 us
  waiting for transfers between devices  479 us (73%)
  local copies, waits for them, and re-layouts  53.3 us (8%)
  matrix products  39.7 us (6%)
  other arithmetic  34.3 us (5%)
  starting transfers between devices  30.6 us (5%)
  between operations  13.8 us (2%)
    psum x1, waiting for transfers between devices, on_device(): gathered = lax.psum(pieces.astype(jnp.bfloat16), 'ctx')  294 us
    all_to_all x1, waiting for transfers between devices, on_device(): lax.all_to_all(partial_out[None], 'ksplit', split_axis=2, concat_axis=0,...  184 us
    ppermute x5, starting transfers between devices, passed_along(): return lax.ppermute(block, axis, route)  16 us
    gather x1, local copies, waits for them, and re-layouts, on_device(): slash_key_value = window_blocks[block_index]  14.1 us
    dot_general x1, matrix products, on_device(): jnp.einsum('rghd,gkd->grhk', grouped_heads, vertical_kv[..., :head_dim],...  13.4 us
  transfers between devices with their start and end apart: 8, of which 3 were waited for; matrix products, arithmetic and copies ran while one was open for 5% of the time, Pallas kernels for 0%

commit v1 on v0

v1 whole, which is shorter than its diff:
```python
import functools
import math

import jax
import jax.numpy as jnp
from jax import lax
from jax.experimental import pallas as pl
from jax.experimental.pallas import tpu as pltpu
from jax.sharding import PartitionSpec as P

MESH = pl.DeviceIdType.MESH
BLOCK = 64
NX = 4
NY = 4
NZ = 8
HOPS = 5
MASKED = -1e30
SCALE = math.log2(math.e) / math.sqrt(128.0)
BAND = 42 * BLOCK
SLASH_CHUNK = 896
F32 = jnp.float32
BF16 = jnp.bfloat16


def iota(shape, dim):
    return lax.broadcasted_iota(jnp.int32, shape, dim)


def kernel(
    q_hbm, s_hbm, p_hbm, vertical, offsets, home, out,
    xq, xs, xp, contrib, r1, p1, r2, fin, zr, vert, win, qb, band, acc, top,
    load_sem, r1_send, r1_recv, r2_send, r2_recv, z_send, z_recv,
    g1_send, g1_recv, g2_send, g2_recv, v_send, v_recv, w_send, w_recv, f_send, f_recv,
):
    c = lax.axis_index("ctx")
    s = lax.axis_index("ksplit")
    x, y = c // NY, c % NY
    z, core = s // 2, s % 2

    load_p = pltpu.make_async_copy(p_hbm, xp, load_sem.at[0])
    load_s = pltpu.make_async_copy(s_hbm, xs, load_sem.at[1])
    slab = pl.multiple_of((s // 8) * 16, 16)
    load_q = pltpu.make_async_copy(q_hbm.at[:, pl.ds(slab, 16), :], xq, load_sem.at[2])
    load_p.start()
    load_s.start()
    load_q.start()

    barrier = pltpu.get_barrier_semaphore()
    for k in range(1, NX * NY):
        pl.semaphore_signal(barrier, inc=1, device_id=((c + k) % (NX * NY), s), device_id_type=MESH)
    for k in range(1, NZ):
        pl.semaphore_signal(barrier, inc=1, device_id=(c, ((z + k) % NZ) * 2 + core), device_id_type=MESH)
    pl.semaphore_signal(barrier, inc=1, device_id=(c, z * 2 + 1 - core), device_id_type=MESH)

    me = c * (2 * NZ) + s
    row16 = iota((16, 256), 0) % 8
    codes = []
    for v in range(4):
        code = jnp.full((16, 256), -1, jnp.int32)
        for g in range(8):
            slot = home[vertical[g, v * 2 * NZ + s]]
            here = jnp.where(slot // 4 == me, slot % 4, -1)
            code = jnp.where(row16 == g, here, code)
        codes.append(code)

    load_p.wait()
    for v in range(4):
        total = None
        for r in range(4):
            keep = jnp.where(codes[v] == r, 1.0, 0.0).astype(BF16)
            term = xp[pl.ds(r * 512, 512), :].reshape(32, 16, 256) * keep[None]
            total = term if total is None else total + term
        contrib[v] = total.reshape(512, 256)

    pl.semaphore_wait(barrier, NX * NY - 1 + NZ - 1 + 1)

    def along_x(k):
        return (((x + k) % NX) * NY + y, s)

    def along_y(k):
        return (x * NY + (y + k) % NY, s)

    sibling = (c, z * 2 + 1 - core)

    def remote(src, dst, send, recv, to):
        return pltpu.make_async_remote_copy(
            src_ref=src, dst_ref=dst, send_sem=send, recv_sem=recv, device_id=to, device_id_type=MESH
        )

    def first_round(half, k):
        to = along_x(k) if half == 0 else along_y(k)
        part = (x + k) % NX if half == 0 else (y + k) % NY
        src = contrib.at[pl.ds(2 * half, 2), pl.ds(pl.multiple_of(part * 128, 128), 128), :]
        return remote(src, r1.at[half, k - 1], r1_send.at[half, k - 1], r1_recv.at[half, k - 1], to)

    def second_round(half, k):
        to = along_y(k) if half == 0 else along_x(k)
        part = (y + k) % NY if half == 0 else (x + k) % NX
        src = p1.at[half, :, pl.ds(pl.multiple_of(part * 32, 32), 32), :]
        return remote(src, r2.at[half, k - 1], r2_send.at[half, k - 1], r2_recv.at[half, k - 1], to)

    order = (2, 1, 3)
    sends = []
    for k in order:
        for half in range(2):
            copy = first_round(half, k)
            copy.start()
            sends.append(copy)

    load_s.wait()
    pick_kv = jnp.where(iota((64, 512), 1) == iota((64, 512), 0) * 8 + z, 1.0, 0.0).astype(BF16)
    for b in range(8):
        picked = jnp.dot(pick_kv, xs[pl.ds(b * 512, 512), :], preferred_element_type=F32)
        win[pl.ds(HOPS * 512 + b * 64, 64), :] = picked.astype(BF16)

    def window_copy(d):
        half = pl.multiple_of(core * 256, 256)
        return remote(
            win.at[pl.ds(HOPS * 512 + half, 256), :],
            win.at[pl.ds((HOPS - d) * 512 + half, 256), :],
            w_send.at[d - 1], w_recv.at[d - 1], ((c + d) % (NX * NY), s),
        )

    def window_swap(d):
        part = win.at[pl.ds((HOPS - d) * 512 + pl.multiple_of(core * 256, 256), 256), :]
        return remote(part, part, f_send.at[d - 1], f_recv.at[d - 1], sibling)

    load_q.wait()
    i, j = iota((128, 1024), 0), iota((128, 1024), 1)
    pick_q = jnp.where(j == (i % 64) * 16 + 2 * (s % 8) + i // 64, 1.0, 0.0).astype(BF16)
    for b in range(8):
        slab_rows = xq[pl.ds(b * 64, 64)].reshape(1024, 128)
        qb[b] = jnp.dot(pick_q, slab_rows, preferred_element_type=F32).astype(BF16)

    rows = iota((8, BAND), 0)
    offset = 40 + (rows // 2) % 2 - iota((8, BAND), 1) // 64
    member = jnp.full((8, BAND), MASKED, F32)
    for n in range(32):
        first, second = offsets[2 * s, n], offsets[2 * s + 1, n]
        member = jnp.where(offset == jnp.where(rows % 2 == 0, first, second), 0.0, member)
    band[...] = member

    for half in range(2):
        part = x if half == 0 else y
        total = contrib[pl.ds(2 * half, 2), pl.ds(pl.multiple_of(part * 128, 128), 128), :]
        for k in order:
            first_round(half, k).wait_recv()
            total = total + r1[half, k - 1]
        p1[half] = total
        for k in order:
            copy = second_round(half, k)
            copy.start()
            sends.append(copy)
    for d in (2, 5, 3, 1, 4):
        copy = window_copy(d)
        copy.start()
        sends.append(copy)

    ends = []
    for half in range(2):
        part = y if half == 0 else x
        total = p1[half, :, pl.ds(pl.multiple_of(part * 32, 32), 32), :]
        for k in order:
            second_round(half, k).wait_recv()
            total = total + r2[half, k - 1]
        ends.append(total.reshape(64, 256))
    held = jnp.concatenate(ends, 0)
    i, j = iota((128, 128), 0), iota((128, 128), 1)
    by_head = jnp.where(i == (j % 8) * 16 + (j // 32) * 4 + (j % 32) // 8, 1.0, 0.0).astype(BF16)
    fin[...] = jnp.dot(by_head, held, preferred_element_type=F32).astype(BF16)

    def z_copy(k):
        there = (z + k) % NZ
        return remote(
            fin.at[pl.ds(pl.multiple_of(there * 16, 16), 16), :],
            zr.at[pl.ds(pl.multiple_of(z * 16, 16), 16), :],
            z_send.at[k - 1], z_recv.at[k - 1], (c, there * 2 + core),
        )

    def z_arrival(k):
        there = (z + NZ - k) % NZ
        place = zr.at[pl.ds(pl.multiple_of(there * 16, 16), 16), :]
        return remote(place, place, z_send.at[k - 1], z_recv.at[k - 1], (c, there * 2 + core))

    for k in (4, 3, 5, 2, 6, 1, 7):
        copy = z_copy(k)
        copy.start()
        sends.append(copy)
    mine = pl.ds(pl.multiple_of(z * 16, 16), 16)
    zr[mine, :] = fin[mine, :]
    for k in range(1, NZ):
        z_arrival(k).wait_recv()

    def place(owner, half, outer, inner, count=64):
        start = ((owner * 2 + half) * 16 + outer * 4 + inner) * 64
        return vert.at[pl.ds(pl.multiple_of(start, 64), count), :]

    def spread_one(half, k):
        outer, inner = (x, y) if half == 0 else (y, x)
        part = place(core, half, outer, inner)
        to = along_y(k) if half == 0 else along_x(k)
        return remote(part, part, g1_send.at[half, k - 1], g1_recv.at[half, k - 1], to)

    def spread_one_arrival(half, k):
        outer, inner = (x, (y + 4 - k) % 4) if half == 0 else (y, (x + 4 - k) % 4)
        part = place(core, half, outer, inner)
        to = along_y(k) if half == 0 else along_x(k)
        return remote(part, part, g1_send.at[half, k - 1], g1_recv.at[half, k - 1], to)

    def spread_two(half, k):
        outer = x if half == 0 else y
        part = place(core, half, outer, 0, 256)
        to = along_x(k) if half == 0 else along_y(k)
        return remote(part, part, g2_send.at[half, k - 1], g2_recv.at[half, k - 1], to)

    def spread_two_arrival(half, k):
        outer = ((x if half == 0 else y) + 4 - k) % 4
        part = place(core, half, outer, 0, 256)
        to = along_x(k) if half == 0 else along_y(k)
        return remote(part, part, g2_send.at[half, k - 1], g2_recv.at[half, k - 1], to)

    def swap(half, k):
        outer = ((x if half == 0 else y) + 4 - k) % 4
        part = place(core, half, outer, 0, 256)
        return remote(part, part, v_send.at[half, k], v_recv.at[half, k], sibling)

    def swap_arrival(half, k):
        outer = ((x if half == 0 else y) + 4 - k) % 4
        part = place(1 - core, half, outer, 0, 256)
        return remote(part, part, v_send.at[half, k], v_recv.at[half, k], sibling)

    for half in range(2):
        outer, inner = (x, y) if half == 0 else (y, x)
        start = pl.multiple_of(((core * 2 + half) * 16 + outer * 4 + inner) * 64, 64)
        vert[pl.ds(start, 64), :] = zr[pl.ds(half * 64, 64), :]
        for k in order:
            copy = spread_one(half, k)
            copy.start()
            sends.append(copy)
    for half in range(2):
        for k in order:
            spread_one_arrival(half, k).wait_recv()
        for k in order:
            copy = spread_two(half, k)
            copy.start()
            sends.append(copy)
        copy = swap(half, 0)
        copy.start()
        sends.append(copy)

    for d in range(1, HOPS + 1):
        window_copy(d).wait_recv()
        copy = window_swap(d)
        copy.start()
        sends.append(copy)
    for d in range(1, HOPS + 1):
        part = win.at[pl.ds((HOPS - d) * 512 + pl.multiple_of((1 - core) * 256, 256), 256), :]
        remote(part, part, f_send.at[d - 1], f_recv.at[d - 1], sibling).wait_recv()

    acc[...] = jnp.zeros(acc.shape, F32)
    top[...] = jnp.full(top.shape, MASKED, F32)
    ones = {}

    def attend(pair, keys, bias, last):
        rows = pl.ds(pl.multiple_of(pair * 256, 256), 256)
        q = qb[pl.ds(pair * 2, 2)].reshape(256, 128)
        n = keys.shape[0]
        scores = lax.dot_general(q, keys[:, :128], (((1,), (1,)), ((), ())), preferred_element_type=F32)
        if bias is not None:
            wide = [jnp.broadcast_to(bias[r : r + 1], (64, n)) for r in range(4)]
            scores = scores + jnp.concatenate(wide, 0)
            if last:
                i, j = iota((256, 128), 0), iota((256, 128), 1)
                later = (j // 64 == i // 128) & (j % 64 > i % 64)
                tail = scores[:, n - 128 :] + jnp.where(later, MASKED, 0.0)
                scores = jnp.concatenate([scores[:, : n - 128], tail], 1)
        old = top[rows, :]
        new = jnp.maximum(old, jnp.max(scores, 1, keepdims=True))
        top[rows, :] = new
        probs = jnp.exp2((scores - new[:, :1]) * SCALE).astype(BF16)
        fade = jnp.exp2((old - new) * SCALE)
        values = jnp.concatenate([keys[:, 128:], jnp.ones((n, 128), BF16)], 1)
        add = jnp.dot(probs, values, preferred_element_type=F32)
        acc[rows, :] = acc[rows, :] * jnp.concatenate([fade, fade], 1) + add

    def slash_pair(pair, _):
        for chunk in range(BAND // SLASH_CHUNK):
            start = pl.multiple_of(pair * 128 + chunk * SLASH_CHUNK, 128)
            lanes = pl.ds(chunk * SLASH_CHUNK, SLASH_CHUNK)
            block = c * 8 - 40 + 2 * pair + (iota((8, SLASH_CHUNK), 1) + chunk * SLASH_CHUNK) // 64
            bias = band[:, lanes] + jnp.where(block >= 0, 0.0, MASKED)
            attend(pair, win[pl.ds(start, SLASH_CHUNK), :], bias, chunk == BAND // SLASH_CHUNK - 1)
        return 0

    lax.fori_loop(0, 4, slash_pair, 0)

    for k in order:
        for half in range(2):
            spread_two_arrival(half, k).wait_recv()
            copy = swap(half, k)
            copy.start()
            sends.append(copy)
    for k in (0,) + order:
        for half in range(2):
            swap_arrival(half, k).wait_recv()

    def vertical_pair(pair, _):
        for chunk in range(4):
            attend(pair, vert[pl.ds(chunk * 1024, 1024), :], None, False)
        return 0

    lax.fori_loop(0, 4, vertical_pair, 0)

    for b in range(8):
        for h in range(2):
            rows = pl.ds(b * 128 + h * 64, 64)
            out[pl.ds(b * 64, 64), pl.ds(h * 128, 128)] = (acc[rows, :128] / acc[rows, 128:]).astype(BF16)

    for copy in sends:
        copy.wait_send()


def on_device(queries, stretch_kv, prefix_kv, vertical, slash_offsets, block_home):
    anywhere = pl.BlockSpec(memory_space=pl.ANY)
    scalars = pl.BlockSpec(memory_space=pltpu.SMEM)
    dma = pltpu.SemaphoreType.DMA
    return pl.pallas_call(
        kernel,
        out_shape=jax.ShapeDtypeStruct((512, 256), BF16),
        in_specs=[anywhere] * 3 + [scalars] * 3,
        out_specs=pl.BlockSpec(memory_space=pltpu.VMEM),
        scratch_shapes=[
            pltpu.VMEM((512, 16, 128), BF16),
            pltpu.VMEM((4096, 256), BF16),
            pltpu.VMEM((2048, 256), BF16),
            pltpu.VMEM((4, 512, 256), BF16),
            pltpu.VMEM((2, 3, 2, 128, 256), BF16),
            pltpu.VMEM((2, 2, 128, 256), BF16),
            pltpu.VMEM((2, 3, 2, 32, 256), BF16),
            pltpu.VMEM((128, 256), BF16),
            pltpu.VMEM((128, 256), BF16),
            pltpu.VMEM((4096, 256), BF16),
            pltpu.VMEM(((HOPS + 1) * 512, 256), BF16),
            pltpu.VMEM((8, 128, 128), BF16),
            pltpu.VMEM((8, BAND), F32),
            pltpu.VMEM((1024, 256), F32),
            pltpu.VMEM((1024, 128), F32),
            dma((3,)),
            dma((2, 3)), dma((2, 3)),
            dma((2, 3)), dma((2, 3)),
            dma((NZ - 1,)), dma((NZ - 1,)),
            dma((2, 3)), dma((2, 3)),
            dma((2, 3)), dma((2, 3)),
            dma((2, 4)), dma((2, 4)),
            dma((HOPS,)), dma((HOPS,)),
            dma((HOPS,)), dma((HOPS,)),
        ],
        compiler_params=pltpu.CompilerParams(
            collective_id=0, has_side_effects=True, vmem_limit_bytes=48 * 1024 * 1024
        ),
        cost_estimate=pl.CostEstimate(flops=7_000_000_000, bytes_accessed=6_000_000, transcendentals=7_000_000),
    )(
        queries,
        stretch_kv.reshape(-1, 256),
        prefix_kv.reshape(-1, 256),
        vertical,
        slash_offsets,
        block_home,
    )


def solution(mesh):
    return jax.shard_map(
        on_device,
        mesh=mesh,
        in_specs=(
            P("ctx", None, None),
            P("ctx", None, None),
            P(("ctx", "ksplit"), None, None, None),
            P(),
            P(),
            P(),
        ),
        out_specs=P("ctx", "ksplit"),
        check_vma=False,
    )
```

time: 652 us -> 62.9 us (0.10)
  the two profiles are of different devices: /device:TPU:4 before, /device:TPU:1 now
where the time goes in v1:
time: 62.9 us; the launch traced here: 61.8 us
  Pallas kernels  56.2 us (89%)
  local copies, waits for them, and re-layouts  5.61 us (9%)
    pallas_call x1, Pallas kernels, on_device(): pl.pallas_call(kernel, out_shape=jax.ShapeDtypeStruct((512, 256), BF16),...  56.2 us
    unnamed x11, local copies, waits for them, and re-layouts  5.61 us

profile of v1, /device:TPU:1, one launch (start us, length us, event | category | flops | bytes accessed | tf_op | source)
XLA Modules:
  0.0 61.8 jit_solution(11263176343917835243)
XLA Ops:
  0.0 0.0 copy-start
  0.0 1.6 %copy-done = bf16[512,8,256]{2,1,0:T(8,128)(2,1)S(1)} copy-done((bf16[512,8,256]{2,1,0:T(8,128)(2,1)S(1)}, bf16[512,8,256]{2,1,0:T(8,128)(2,1)}, u32[]{:S(2)}) %copy-start) | copy-done | bytes 2097176
  1.6 0.0 copy-start.1
  1.6 1.2 %copy-done.1 = bf16[4,64,8,256]{3,2,1,0:T(8,128)(2,1)S(1)} copy-done((bf16[4,64,8,256]{3,2,1,0:T(8,128)(2,1)S(1)}, bf16[4,64,8,256]{3,2,1,0:T(8,128)(2,1)}, u32[]{:S(2)}) %copy-start.1) | copy-done | bytes 1048600
  2.8 0.0 copy-start.2
  2.8 0.7 %copy-done.2 = s32[32,32]{1,0:T(8,128)S(1)} copy-done((s32[32,32]{1,0:T(8,128)S(1)}, s32[32,32]{1,0:T(8,128)}, u32[]{:S(2)}) %copy-start.2) | copy-done | bytes 4120
  3.5 0.0 copy-start.3
  3.5 0.7 %copy-done.3 = s32[8,64]{1,0:T(8,128)S(1)} copy-done((s32[8,64]{1,0:T(8,128)S(1)}, s32[8,64]{1,0:T(8,128)}, u32[]{:S(2)}) %copy-start.3) | copy-done | bytes 2072
  4.2 0.0 copy-start.4
  4.2 0.7 %copy-done.4 = s32[1024]{0:T(1024)S(1)} copy-done((s32[1024]{0:T(1024)S(1)}, s32[1024]{0:T(1024)}, u32[]{:S(2)}) %copy-start.4) | copy-done | bytes 4120
  4.9 56.2 %shard_map.64 = bf16[512,256]{1,0:T(8,128)(2,1)S(1)} custom-call(bf16[512,32,128]{2,1,0:T(8,128)(2,1)} %q_hbm.1, bf16[4096,256]{1,0:T(8,128)(2,1)S(1)} %bitcast.2, bf16[2048,256]{1,0:T(8,128)(2,1)S(1)} %bitcast.3, s32[8,64]{1,0:T(8,128)S(1)} %copy-done.3, s32[32,32]{1,0:T(8,128)S(1)} %copy-done.2, s32[1024]{0:T(1024)S(1)} %copy-done.4), custom_call_target="tpu_custom_call" | custom-call | flops 7000000000 | bytes 6000000 | tf_op jit(solution)/shard_map/pallas_call | solution.py:327
  61.1 0.7 %copy.8 = bf16[512,256]{1,0:T(8,128)(2,1)} copy(bf16[512,256]{1,0:T(8,128)(2,1)S(1)} %shard_map.64) | data formatting | bytes 524288
Async XLA Ops:
  0.0 1.6 %copy-start = (bf16[512,8,256]{2,1,0:T(8,128)(2,1)S(1)}, bf16[512,8,256]{2,1,0:T(8,128)(2,1)}, u32[]{:S(2)}) copy-start(bf16[512,8,256]{2,1,0:T(8,128)(2,1)} %param.7) | copy-start | bytes 6291460
  1.6 1.2 %copy-start.1 = (bf16[4,64,8,256]{3,2,1,0:T(8,128)(2,1)S(1)}, bf16[4,64,8,256]{3,2,1,0:T(8,128)(2,1)}, u32[]{:S(2)}) copy-start(bf16[4,64,8,256]{3,2,1,0:T(8,128)(2,1)} %param.8) | copy-start | bytes 3145732
  2.8 0.7 %copy-start.2 = (s32[32,32]{1,0:T(8,128)S(1)}, s32[32,32]{1,0:T(8,128)}, u32[]{:S(2)}) copy-start(s32[32,32]{1,0:T(8,128)} %offsets.1) | copy-start | bytes 12292
  3.5 0.7 %copy-start.3 = (s32[8,64]{1,0:T(8,128)S(1)}, s32[8,64]{1,0:T(8,128)}, u32[]{:S(2)}) copy-start(s32[8,64]{1,0:T(8,128)} %vertical.1) | copy-start | bytes 6148
  4.2 0.7 %copy-start.4 = (s32[1024]{0:T(1024)S(1)}, s32[1024]{0:T(1024)}, u32[]{:S(2)}) copy-start(s32[1024]{0:T(1024)} %home.1) | copy-start | bytes 12292

commit v2 on v1

--- a/solution.py
+++ b/solution.py
@@ -17,7 +17,6 @@
 MASKED = -1e30
 SCALE = math.log2(math.e) / math.sqrt(128.0)
 BAND = 42 * BLOCK
-SLASH_CHUNK = 896
 F32 = jnp.float32
 BF16 = jnp.bfloat16
 
@@ -37,6 +36,14 @@
     x, y = c // NY, c % NY
     z, core = s // 2, s % 2
 
+    barrier = pltpu.get_barrier_semaphore()
+    for k in range(1, 4):
+        pl.semaphore_signal(barrier, inc=1, device_id=(((x + k) % NX) * NY + y, s), device_id_type=MESH)
+        pl.semaphore_signal(barrier, inc=1, device_id=(x * NY + (y + k) % NY, s), device_id_type=MESH)
+    for k in range(1, NZ):
+        pl.semaphore_signal(barrier, inc=1, device_id=(c, ((z + k) % NZ) * 2 + core), device_id_type=MESH)
+    pl.semaphore_signal(barrier, inc=1, device_id=(c, z * 2 + 1 - core), device_id_type=MESH)
+
     load_p = pltpu.make_async_copy(p_hbm, xp, load_sem.at[0])
     load_s = pltpu.make_async_copy(s_hbm, xs, load_sem.at[1])
     slab = pl.multiple_of((s // 8) * 16, 16)
@@ -44,13 +51,6 @@
     load_p.start()
     load_s.start()
     load_q.start()
-
-    barrier = pltpu.get_barrier_semaphore()
-    for k in range(1, NX * NY):
-        pl.semaphore_signal(barrier, inc=1, device_id=((c + k) % (NX * NY), s), device_id_type=MESH)
-    for k in range(1, NZ):
-        pl.semaphore_signal(barrier, inc=1, device_id=(c, ((z + k) % NZ) * 2 + core), device_id_type=MESH)
-    pl.semaphore_signal(barrier, inc=1, device_id=(c, z * 2 + 1 - core), device_id_type=MESH)
 
     me = c * (2 * NZ) + s
     row16 = iota((16, 256), 0) % 8
@@ -72,7 +72,7 @@
             total = term if total is None else total + term
         contrib[v] = total.reshape(512, 256)
 
-    pl.semaphore_wait(barrier, NX * NY - 1 + NZ - 1 + 1)
+    pl.semaphore_wait(barrier, 3 + 3 + NZ - 1 + 1)
 
     def along_x(k):
         return (((x + k) % NX) * NY + y, s)
@@ -113,16 +113,18 @@
         picked = jnp.dot(pick_kv, xs[pl.ds(b * 512, 512), :], preferred_element_type=F32)
         win[pl.ds(HOPS * 512 + b * 64, 64), :] = picked.astype(BF16)
 
-    def window_copy(d):
-        half = pl.multiple_of(core * 256, 256)
-        return remote(
-            win.at[pl.ds(HOPS * 512 + half, 256), :],
-            win.at[pl.ds((HOPS - d) * 512 + half, 256), :],
-            w_send.at[d - 1], w_recv.at[d - 1], ((c + d) % (NX * NY), s),
-        )
-
-    def window_swap(d):
-        part = win.at[pl.ds((HOPS - d) * 512 + pl.multiple_of(core * 256, 256), 256), :]
+    def window_part(d, which):
+        return win.at[pl.ds(pl.multiple_of((HOPS - d) * 512 + which * 256, 256), 256), :]
+
+    def window_copy(d, held):
+        to = along_x(1) if d >= 4 else along_y(d)
+        return remote(window_part(held, core), window_part(d, core), w_send.at[d - 1], w_recv.at[d - 1], to)
+
+    def window_arrival(d):
+        return window_copy(d, d)
+
+    def window_swap(d, which):
+        part = window_part(d, which)
         return remote(part, part, f_send.at[d - 1], f_recv.at[d - 1], sibling)
 
     load_q.wait()
@@ -151,10 +153,15 @@
             copy = second_round(half, k)
             copy.start()
             sends.append(copy)
-    for d in (2, 5, 3, 1, 4):
-        copy = window_copy(d)
-        copy.start()
-        sends.append(copy)
+    copy = window_copy(4, 0)
+    copy.start()
+    sends.append(copy)
+    for d in (1, 2, 3):
+
+        @pl.when(y + d < NY)
+        def _(d=d):
+            window_copy(d, 0).start()
+
 
     ends = []
     for half in range(2):
@@ -186,130 +193,158 @@
         copy = z_copy(k)
         copy.start()
         sends.append(copy)
+    window_arrival(4).wait_recv()
+    for d in (1, 2, 3):
+
+        @pl.when(y + d >= NY)
+        def _(d=d):
+            window_copy(d, 4).start()
+
+        sends.append(window_copy(d, 0))
+    copy = window_swap(4, core)
+    copy.start()
+    sends.append(copy)
     mine = pl.ds(pl.multiple_of(z * 16, 16), 16)
     zr[mine, :] = fin[mine, :]
     for k in range(1, NZ):
         z_arrival(k).wait_recv()
 
-    def place(owner, half, outer, inner, count=64):
-        start = ((owner * 2 + half) * 16 + outer * 4 + inner) * 64
-        return vert.at[pl.ds(pl.multiple_of(start, 64), count), :]
+    def place(k, owner, half, start, count):
+        return vert.at[pl.ds(pl.multiple_of(((k * 2 + owner) * 2 + half) * 256 + start, 64), count), :]
 
     def spread_one(half, k):
-        outer, inner = (x, y) if half == 0 else (y, x)
-        part = place(core, half, outer, inner)
         to = along_y(k) if half == 0 else along_x(k)
-        return remote(part, part, g1_send.at[half, k - 1], g1_recv.at[half, k - 1], to)
-
-    def spread_one_arrival(half, k):
-        outer, inner = (x, (y + 4 - k) % 4) if half == 0 else (y, (x + 4 - k) % 4)
-        part = place(core, half, outer, inner)
-        to = along_y(k) if half == 0 else along_x(k)
-        return remote(part, part, g1_send.at[half, k - 1], g1_recv.at[half, k - 1], to)
+        dst = place(0, core, half, k * 64, 64)
+        return remote(place(0, core, half, 0, 64), dst, g1_send.at[half, k - 1], g1_recv.at[half, k - 1], to)
 
     def spread_two(half, k):
-        outer = x if half == 0 else y
-        part = place(core, half, outer, 0, 256)
         to = along_x(k) if half == 0 else along_y(k)
-        return remote(part, part, g2_send.at[half, k - 1], g2_recv.at[half, k - 1], to)
-
-    def spread_two_arrival(half, k):
-        outer = ((x if half == 0 else y) + 4 - k) % 4
-        part = place(core, half, outer, 0, 256)
-        to = along_x(k) if half == 0 else along_y(k)
-        return remote(part, part, g2_send.at[half, k - 1], g2_recv.at[half, k - 1], to)
-
-    def swap(half, k):
-        outer = ((x if half == 0 else y) + 4 - k) % 4
-        part = place(core, half, outer, 0, 256)
+        dst = place(k, core, half, 0, 256)
+        return remote(place(0, core, half, 0, 256), dst, g2_send.at[half, k - 1], g2_recv.at[half, k - 1], to)
+
+    def swap(half, k, owner):
+        part = place(k, owner, half, 0, 256)
         return remote(part, part, v_send.at[half, k], v_recv.at[half, k], sibling)
 
-    def swap_arrival(half, k):
-        outer = ((x if half == 0 else y) + 4 - k) % 4
-        part = place(1 - core, half, outer, 0, 256)
-        return remote(part, part, v_send.at[half, k], v_recv.at[half, k], sibling)
+    def start_swap(k):
+        for half in range(2):
+            copy = swap(half, k, core)
+            copy.start()
+            sends.append(copy)
+
+    def end_swap(k):
+        for half in range(2):
+            swap(half, k, 1 - core).wait_recv()
+
+    def arrive(k):
+        for half in range(2):
+            spread_two(half, k).wait_recv()
+        start_swap(k)
 
     for half in range(2):
-        outer, inner = (x, y) if half == 0 else (y, x)
-        start = pl.multiple_of(((core * 2 + half) * 16 + outer * 4 + inner) * 64, 64)
+        start = pl.multiple_of((core * 2 + half) * 256, 256)
         vert[pl.ds(start, 64), :] = zr[pl.ds(half * 64, 64), :]
         for k in order:
             copy = spread_one(half, k)
             copy.start()
             sends.append(copy)
+
+    def attend(b, keys, bias=None, diagonal=False, first=False):
+        rows = pl.ds(b * 128, 128)
+        n = keys.shape[0]
+        scores = lax.dot_general(qb[b], keys[:, :128], (((1,), (1,)), ((), ())), preferred_element_type=F32)
+        if bias is not None:
+            wide = [jnp.broadcast_to(bias[r : r + 1], (64, n)) for r in (2 * (b % 2), 2 * (b % 2) + 1)]
+            scores = scores + jnp.concatenate(wide, 0)
+        if diagonal:
+            i, j = iota((128, 128), 0), iota((128, 128), 1)
+            later = (j // 64 == b % 2) & (j % 64 > i % 64)
+            tail = scores[:, n - 128 :] + jnp.where(later, MASKED, 0.0)
+            scores = jnp.concatenate([scores[:, : n - 128], tail], 1)
+        new = jnp.max(scores, 1, keepdims=True)
+        if not first:
+            old = top[rows, :]
+            new = jnp.maximum(old, new)
+        probs = jnp.exp2((scores - new[:, :1]) * SCALE).astype(BF16)
+        values = jnp.concatenate([keys[:, 128:], jnp.ones((n, 128), BF16)], 1)
+        add = jnp.dot(probs, values, preferred_element_type=F32)
+        if first:
+            top[rows, :] = jnp.broadcast_to(new, (128, 128))
+            acc[rows, :] = add
+        else:
+            fade = jnp.exp2((old - new) * SCALE)
+            top[rows, :] = new
+            acc[rows, :] = acc[rows, :] * jnp.concatenate([fade, fade], 1) + add
+
+    def band_part(start, count, d):
+        return band[:, pl.ds(start, count)] + jnp.where(c >= d, 0.0, MASKED)
+
+    def slash_near():
+        for b in range(8):
+            p = b // 2
+            keys = jnp.concatenate([win[pl.ds(512, 512), :], win[pl.ds(2560, 128 * p + 128), :]], 0)
+            bias = [band_part(512 - 128 * p, 512, 4), band_part(2560 - 128 * p, 128 * p + 128, 0)]
+            attend(b, keys, jnp.concatenate(bias, 1), diagonal=True, first=True)
+
+    def slash_middle():
+        for b in range(8):
+            p = b // 2
+            bias = [band_part(1024 - 128 * p, 512, 3), band_part(1536 - 128 * p, 512, 2)]
+            attend(b, win[pl.ds(1024, 1024), :], jnp.concatenate(bias, 1))
+
+    def slash_far():
+        for b in range(8):
+            p = b // 2
+            keys = jnp.concatenate([win[pl.ds(128 * p, 512 - 128 * p), :], win[pl.ds(2048, 512), :]], 0)
+            bias = [band_part(0, 512 - 128 * p, 5), band_part(2048 - 128 * p, 512, 1)]
+            attend(b, keys, jnp.concatenate(bias, 1))
+
+    def vertical_step(k):
+        for b in range(8):
+            attend(b, vert[pl.ds(k * 1024, 1024), :])
+
+    window_swap(4, 1 - core).wait_recv()
+    slash_near()
+
     for half in range(2):
         for k in order:
-            spread_one_arrival(half, k).wait_recv()
-        for k in order:
+            spread_one(half, k).wait_recv()
+        for k in (1, 3, 2):
             copy = spread_two(half, k)
             copy.start()
             sends.append(copy)
-        copy = swap(half, 0)
+    start_swap(0)
+    for d in (1, 2, 3):
+        window_arrival(d).wait_recv()
+        if d == 1:
+            copy = window_copy(5, 1)
+            copy.start()
+            sends.append(copy)
+        copy = window_swap(d, core)
         copy.start()
         sends.append(copy)
 
-    for d in range(1, HOPS + 1):
-        window_copy(d).wait_recv()
-        copy = window_swap(d)
-        copy.start()
-        sends.append(copy)
-    for d in range(1, HOPS + 1):
-        part = win.at[pl.ds((HOPS - d) * 512 + pl.multiple_of((1 - core) * 256, 256), 256), :]
-        remote(part, part, f_send.at[d - 1], f_recv.at[d - 1], sibling).wait_recv()
-
-    acc[...] = jnp.zeros(acc.shape, F32)
-    top[...] = jnp.full(top.shape, MASKED, F32)
-    ones = {}
-
-    def attend(pair, keys, bias, last):
-        rows = pl.ds(pl.multiple_of(pair * 256, 256), 256)
-        q = qb[pl.ds(pair * 2, 2)].reshape(256, 128)
-        n = keys.shape[0]
-        scores = lax.dot_general(q, keys[:, :128], (((1,), (1,)), ((), ())), preferred_element_type=F32)
-        if bias is not None:
-            wide = [jnp.broadcast_to(bias[r : r + 1], (64, n)) for r in range(4)]
-            scores = scores + jnp.concatenate(wide, 0)
-            if last:
-                i, j = iota((256, 128), 0), iota((256, 128), 1)
-                later = (j // 64 == i // 128) & (j % 64 > i % 64)
-                tail = scores[:, n - 128 :] + jnp.where(later, MASKED, 0.0)
-                scores = jnp.concatenate([scores[:, : n - 128], tail], 1)
-        old = top[rows, :]
-        new = jnp.maximum(old, jnp.max(scores, 1, keepdims=True))
-        top[rows, :] = new
-        probs = jnp.exp2((scores - new[:, :1]) * SCALE).astype(BF16)
-        fade = jnp.exp2((old - new) * SCALE)
-        values = jnp.concatenate([keys[:, 128:], jnp.ones((n, 128), BF16)], 1)
-        add = jnp.dot(probs, values, preferred_element_type=F32)
-        acc[rows, :] = acc[rows, :] * jnp.concatenate([fade, fade], 1) + add
-
-    def slash_pair(pair, _):
-        for chunk in range(BAND // SLASH_CHUNK):
-            start = pl.multiple_of(pair * 128 + chunk * SLASH_CHUNK, 128)
-            lanes = pl.ds(chunk * SLASH_CHUNK, SLASH_CHUNK)
-            block = c * 8 - 40 + 2 * pair + (iota((8, SLASH_CHUNK), 1) + chunk * SLASH_CHUNK) // 64
-            bias = band[:, lanes] + jnp.where(block >= 0, 0.0, MASKED)
-            attend(pair, win[pl.ds(start, SLASH_CHUNK), :], bias, chunk == BAND // SLASH_CHUNK - 1)
-        return 0
-
-    lax.fori_loop(0, 4, slash_pair, 0)
-
-    for k in order:
-        for half in range(2):
-            spread_two_arrival(half, k).wait_recv()
-            copy = swap(half, k)
-            copy.start()
-            sends.append(copy)
-    for k in (0,) + order:
-        for half in range(2):
-            swap_arrival(half, k).wait_recv()
-
-    def vertical_pair(pair, _):
-        for chunk in range(4):
-            attend(pair, vert[pl.ds(chunk * 1024, 1024), :], None, False)
-        return 0
-
-    lax.fori_loop(0, 4, vertical_pair, 0)
+    for d in (2, 3):
+        window_swap(d, 1 - core).wait_recv()
+    slash_middle()
+    end_swap(0)
+    vertical_step(0)
+    arrive(1)
+    arrive(3)
+    window_arrival(5).wait_recv()
+    copy = window_swap(5, core)
+    copy.start()
+    sends.append(copy)
+    end_swap(1)
+    vertical_step(1)
+    for d in (1, 5):
+        window_swap(d, 1 - core).wait_recv()
+    slash_far()
+    arrive(2)
+    end_swap(3)
+    vertical_step(3)
+    end_swap(2)
+    vertical_step(2)
 
     for b in range(8):
         for h in range(2):
@@ -356,7 +391,7 @@
             dma((HOPS,)), dma((HOPS,)),
         ],
         compiler_params=pltpu.CompilerParams(
-            collective_id=0, has_side_effects=True, vmem_limit_bytes=48 * 1024 * 1024
+            collective_id=0, has_side_effects=True, vmem_limit_bytes=62 * 1024 * 1024
         ),
         cost_estimate=pl.CostEstimate(flops=7_000_000_000, bytes_accessed=6_000_000, transcendentals=7_000_000),
     )(

time: 62.9 us -> 53.2 us (0.85); the launches traced: 61.8 us -> 53 us
  Pallas kernels: 56.2 us -> 51.3 us
  local copies, waits for them, and re-layouts: 5.61 us -> 1.67 us
    pallas_call x1, Pallas kernels: 56.2 us -> 51.3 us  [on_device(): pl.pallas_call(kernel, out_shape=jax.ShapeDtypeStruct((512, 256), BF16),...]
    unnamed x11 -> x1, local copies, waits for them, and re-layouts: 5.61 us -> 1.67 us
where the time goes in v2:
time: 53.2 us; the launch traced here: 53 us
  Pallas kernels  51.3 us (96%)
  local copies, waits for them, and re-layouts  1.67 us (3%)
    pallas_call x1, Pallas kernels, on_device(): pl.pallas_call(kernel, out_shape=jax.ShapeDtypeStruct((512, 256), BF16),...  51.3 us
    unnamed x1, local copies, waits for them, and re-layouts  1.67 us

profile of v2, /device:TPU:1, one launch (start us, length us, event | category | flops | bytes accessed | tf_op | source)
XLA Modules:
  0.0 53.0 jit_solution(8755434452533401072)
XLA Ops:
  0.0 51.3 %shard_map.64 = bf16[512,256]{1,0:T(8,128)(2,1)} custom-call(bf16[512,32,128]{2,1,0:T(8,128)(2,1)} %q_hbm.1, bf16[4096,256]{1,0:T(8,128)(2,1)} %bitcast.2, bf16[2048,256]{1,0:T(8,128)(2,1)} %bitcast.3, s32[8,64]{1,0:T(8,128)} %vertical.1, s32[32,32]{1,0:T(8,128)} %offsets.1, s32[1024]{0:T(1024)} %home.1), custom_call_target="tpu_custom_call" | custom-call | flops 7000000000 | bytes 6000000 | tf_op jit(solution)/shard_map/pallas_call | solution.py:362
  51.3 1.7 %copy.8 = bf16[512,256]{1,0:T(8,128)(2,1)} copy(bf16[512,256]{1,0:T(8,128)(2,1)} %shard_map.64) | data formatting | bytes 524288

commit v3 on v2

--- a/solution.py
+++ b/solution.py
@@ -26,8 +26,8 @@
 
 
 def kernel(
-    q_hbm, s_hbm, p_hbm, vertical, offsets, home, out,
-    xq, xs, xp, contrib, r1, p1, r2, fin, zr, vert, win, qb, band, acc, top,
+    q_hbm, s_hbm, p_hbm, vertical_hbm, offsets_hbm, home_hbm, out,
+    vertical, offsets, home, xq, xs, xp, contrib, r1, p1, r2, fin, zr, vert, win, qb, band, acc, top,
     load_sem, r1_send, r1_recv, r2_send, r2_recv, z_send, z_recv,
     g1_send, g1_recv, g2_send, g2_recv, v_send, v_recv, w_send, w_recv, f_send, f_recv,
 ):
@@ -48,10 +48,19 @@
     load_s = pltpu.make_async_copy(s_hbm, xs, load_sem.at[1])
     slab = pl.multiple_of((s // 8) * 16, 16)
     load_q = pltpu.make_async_copy(q_hbm.at[:, pl.ds(slab, 16), :], xq, load_sem.at[2])
+    load_home = pltpu.make_async_copy(home_hbm, home, load_sem.at[3])
+    load_vertical = pltpu.make_async_copy(vertical_hbm, vertical, load_sem.at[4])
+    load_offsets = pltpu.make_async_copy(offsets_hbm, offsets, load_sem.at[5])
+    load_home.start()
+    load_vertical.start()
+    load_offsets.start()
     load_p.start()
     load_s.start()
     load_q.start()
 
+    load_home.wait()
+    load_vertical.wait()
+    load_offsets.wait()
     me = c * (2 * NZ) + s
     row16 = iota((16, 256), 0) % 8
     codes = []
@@ -103,9 +112,7 @@
     sends = []
     for k in order:
         for half in range(2):
-            copy = first_round(half, k)
-            copy.start()
-            sends.append(copy)
+            first_round(half, k).start()
 
     load_s.wait()
     pick_kv = jnp.where(iota((64, 512), 1) == iota((64, 512), 0) * 8 + z, 1.0, 0.0).astype(BF16)
@@ -143,6 +150,9 @@
     band[...] = member
 
     for half in range(2):
+        for k in order:
+            first_round(half, k).wait_send()
+    for half in range(2):
         part = x if half == 0 else y
         total = contrib[pl.ds(2 * half, 2), pl.ds(pl.multiple_of(part * 128, 128), 128), :]
         for k in order:
@@ -156,12 +166,6 @@
     copy = window_copy(4, 0)
     copy.start()
     sends.append(copy)
-    for d in (1, 2, 3):
-
-        @pl.when(y + d < NY)
-        def _(d=d):
-            window_copy(d, 0).start()
-
 
     ends = []
     for half in range(2):
@@ -193,17 +197,6 @@
         copy = z_copy(k)
         copy.start()
         sends.append(copy)
-    window_arrival(4).wait_recv()
-    for d in (1, 2, 3):
-
-        @pl.when(y + d >= NY)
-        def _(d=d):
-            window_copy(d, 4).start()
-
-        sends.append(window_copy(d, 0))
-    copy = window_swap(4, core)
-    copy.start()
-    sends.append(copy)
     mine = pl.ds(pl.multiple_of(z * 16, 16), 16)
     zr[mine, :] = fin[mine, :]
     for k in range(1, NZ):
@@ -249,6 +242,14 @@
             copy.start()
             sends.append(copy)
 
+    window_arrival(4).wait_recv()
+    for d in (1, 2, 3):
+        copy = window_copy(d, jnp.where(y + d < NY, 0, 4))
+        copy.start()
+        sends.append(copy)
+    copy = window_swap(4, core)
+    copy.start()
+    sends.append(copy)
     def attend(b, keys, bias=None, diagonal=False, first=False):
         rows = pl.ds(b * 128, 128)
         n = keys.shape[0]
@@ -289,15 +290,13 @@
     def slash_middle():
         for b in range(8):
             p = b // 2
-            bias = [band_part(1024 - 128 * p, 512, 3), band_part(1536 - 128 * p, 512, 2)]
-            attend(b, win[pl.ds(1024, 1024), :], jnp.concatenate(bias, 1))
+            bias = [band_part((1 + i) * 512 + 512 - 128 * p, 512, 3 - i) for i in range(3)]
+            attend(b, win[pl.ds(1024, 1536), :], jnp.concatenate(bias, 1))
 
     def slash_far():
         for b in range(8):
             p = b // 2
-            keys = jnp.concatenate([win[pl.ds(128 * p, 512 - 128 * p), :], win[pl.ds(2048, 512), :]], 0)
-            bias = [band_part(0, 512 - 128 * p, 5), band_part(2048 - 128 * p, 512, 1)]
-            attend(b, keys, jnp.concatenate(bias, 1))
+            attend(b, win[pl.ds(128 * p, 512 - 128 * p), :], band_part(0, 512 - 128 * p, 5))
 
     def vertical_step(k):
         for b in range(8):
@@ -314,35 +313,34 @@
             copy.start()
             sends.append(copy)
     start_swap(0)
-    for d in (1, 2, 3):
-        window_arrival(d).wait_recv()
-        if d == 1:
-            copy = window_copy(5, 1)
-            copy.start()
-            sends.append(copy)
+    window_arrival(1).wait_recv()
+    copy = window_copy(5, 1)
+    copy.start()
+    sends.append(copy)
+    end_swap(0)
+    vertical_step(0)
+    for d in (1, 3, 2):
+        if d > 1:
+            window_arrival(d).wait_recv()
         copy = window_swap(d, core)
         copy.start()
         sends.append(copy)
-
-    for d in (2, 3):
+    arrive(1)
+    arrive(3)
+    for d in (1, 2, 3):
         window_swap(d, 1 - core).wait_recv()
     slash_middle()
-    end_swap(0)
-    vertical_step(0)
-    arrive(1)
-    arrive(3)
+    end_swap(1)
+    vertical_step(1)
     window_arrival(5).wait_recv()
     copy = window_swap(5, core)
     copy.start()
     sends.append(copy)
-    end_swap(1)
-    vertical_step(1)
-    for d in (1, 5):
-        window_swap(d, 1 - core).wait_recv()
-    slash_far()
     arrive(2)
     end_swap(3)
     vertical_step(3)
+    window_swap(5, 1 - core).wait_recv()
+    slash_far()
     end_swap(2)
     vertical_step(2)
 
@@ -357,14 +355,16 @@
 
 def on_device(queries, stretch_kv, prefix_kv, vertical, slash_offsets, block_home):
     anywhere = pl.BlockSpec(memory_space=pl.ANY)
-    scalars = pl.BlockSpec(memory_space=pltpu.SMEM)
     dma = pltpu.SemaphoreType.DMA
     return pl.pallas_call(
         kernel,
         out_shape=jax.ShapeDtypeStruct((512, 256), BF16),
-        in_specs=[anywhere] * 3 + [scalars] * 3,
+        in_specs=[anywhere] * 6,
         out_specs=pl.BlockSpec(memory_space=pltpu.VMEM),
         scratch_shapes=[
+            pltpu.SMEM((8, 64), jnp.int32),
+            pltpu.SMEM((32, 32), jnp.int32),
+            pltpu.SMEM((1024,), jnp.int32),
             pltpu.VMEM((512, 16, 128), BF16),
             pltpu.VMEM((4096, 256), BF16),
             pltpu.VMEM((2048, 256), BF16),
@@ -380,7 +380,7 @@
             pltpu.VMEM((8, BAND), F32),
             pltpu.VMEM((1024, 256), F32),
             pltpu.VMEM((1024, 128), F32),
-            dma((3,)),
+            dma((6,)),
             dma((2, 3)), dma((2, 3)),
             dma((2, 3)), dma((2, 3)),
             dma((NZ - 1,)), dma((NZ - 1,)),

time: 53.2 us -> 50.6 us (0.951)
  Pallas kernels: 51.3 us -> 48.8 us
    pallas_call x1, Pallas kernels: 51.3 us -> 48.8 us  [on_device(): pl.pallas_call(kernel, out_shape=jax.ShapeDtypeStruct((512, 256), BF16),...]
where the time goes in v3:
time: 50.6 us; the launch traced here: 50.5 us
  Pallas kernels  48.8 us (96%)
  local copies, waits for them, and re-layouts  1.67 us (3%)
    pallas_call x1, Pallas kernels, on_device(): pl.pallas_call(kernel, out_shape=jax.ShapeDtypeStruct((512, 256), BF16),...  48.8 us
    unnamed x1, local copies, waits for them, and re-layouts  1.67 us

profile of v3, /device:TPU:1, one launch (start us, length us, event | category | flops | bytes accessed | tf_op | source)
XLA Modules:
  0.0 50.5 jit_solution(7883390824817686094)
XLA Ops:
  0.0 48.8 %shard_map.64 = bf16[512,256]{1,0:T(8,128)(2,1)} custom-call(bf16[512,32,128]{2,1,0:T(8,128)(2,1)} %q_hbm.1, bf16[4096,256]{1,0:T(8,128)(2,1)} %bitcast.2, bf16[2048,256]{1,0:T(8,128)(2,1)} %bitcast.3, s32[8,64]{1,0:T(8,128)} %vertical_hbm.1, s32[32,32]{1,0:T(8,128)} %offsets_hbm.1, s32[1024]{0:T(1024)} %home_hbm.1), custom_call_target="tpu_custom_call" | custom-call | flops 7000000000 | bytes 6000000 | tf_op jit(solution)/shard_map/pallas_call | solution.py:359
  48.8 1.7 %copy.8 = bf16[512,256]{1,0:T(8,128)(2,1)} copy(bf16[512,256]{1,0:T(8,128)(2,1)} %shard_map.64) | data formatting | bytes 524288

commit v4 on v3

--- a/solution.py
+++ b/solution.py
@@ -152,6 +152,9 @@
     for half in range(2):
         for k in order:
             first_round(half, k).wait_send()
+    copy = window_copy(4, 0)
+    copy.start()
+    sends.append(copy)
     for half in range(2):
         part = x if half == 0 else y
         total = contrib[pl.ds(2 * half, 2), pl.ds(pl.multiple_of(part * 128, 128), 128), :]
@@ -163,9 +166,6 @@
             copy = second_round(half, k)
             copy.start()
             sends.append(copy)
-    copy = window_copy(4, 0)
-    copy.start()
-    sends.append(copy)
 
     ends = []
     for half in range(2):
@@ -197,11 +197,6 @@
         copy = z_copy(k)
         copy.start()
         sends.append(copy)
-    mine = pl.ds(pl.multiple_of(z * 16, 16), 16)
-    zr[mine, :] = fin[mine, :]
-    for k in range(1, NZ):
-        z_arrival(k).wait_recv()
-
     def place(k, owner, half, start, count):
         return vert.at[pl.ds(pl.multiple_of(((k * 2 + owner) * 2 + half) * 256 + start, 64), count), :]
 
@@ -234,22 +229,6 @@
             spread_two(half, k).wait_recv()
         start_swap(k)
 
-    for half in range(2):
-        start = pl.multiple_of((core * 2 + half) * 256, 256)
-        vert[pl.ds(start, 64), :] = zr[pl.ds(half * 64, 64), :]
-        for k in order:
-            copy = spread_one(half, k)
-            copy.start()
-            sends.append(copy)
-
-    window_arrival(4).wait_recv()
-    for d in (1, 2, 3):
-        copy = window_copy(d, jnp.where(y + d < NY, 0, 4))
-        copy.start()
-        sends.append(copy)
-    copy = window_swap(4, core)
-    copy.start()
-    sends.append(copy)
     def attend(b, keys, bias=None, diagonal=False, first=False):
         rows = pl.ds(b * 128, 128)
         n = keys.shape[0]
@@ -290,21 +269,55 @@
     def slash_middle():
         for b in range(8):
             p = b // 2
-            bias = [band_part((1 + i) * 512 + 512 - 128 * p, 512, 3 - i) for i in range(3)]
-            attend(b, win[pl.ds(1024, 1536), :], jnp.concatenate(bias, 1))
+            bias = [band_part(1024 - 128 * p, 512, 3), band_part(1536 - 128 * p, 512, 2)]
+            attend(b, win[pl.ds(1024, 1024), :], jnp.concatenate(bias, 1))
 
     def slash_far():
         for b in range(8):
             p = b // 2
-            attend(b, win[pl.ds(128 * p, 512 - 128 * p), :], band_part(0, 512 - 128 * p, 5))
+            keys = jnp.concatenate([win[pl.ds(128 * p, 512 - 128 * p), :], win[pl.ds(2048, 512), :]], 0)
+            bias = [band_part(0, 512 - 128 * p, 5), band_part(2048 - 128 * p, 512, 1)]
+            attend(b, keys, jnp.concatenate(bias, 1))
 
     def vertical_step(k):
         for b in range(8):
             attend(b, vert[pl.ds(k * 1024, 1024), :])
 
+    window_arrival(4).wait_recv()
+    copy = window_copy(1, jnp.where(y + 1 < NY, 0, 4))
+    copy.start()
+    sends.append(copy)
+    copy = window_copy(3, jnp.where(y + 3 < NY, 0, 4))
+    copy.start()
+    sends.append(copy)
+    copy = window_swap(4, core)
+    copy.start()
+    sends.append(copy)
+    mine = pl.ds(pl.multiple_of(z * 16, 16), 16)
+    zr[mine, :] = fin[mine, :]
+    for k in range(1, NZ):
+        z_arrival(k).wait_recv()
+
+    for half in range(2):
+        start = pl.multiple_of((core * 2 + half) * 256, 256)
+        vert[pl.ds(start, 64), :] = zr[pl.ds(half * 64, 64), :]
+        for k in order:
+            copy = spread_one(half, k)
+            copy.start()
+            sends.append(copy)
+
+    copy = window_copy(2, jnp.where(y + 2 < NY, 0, 4))
+    copy.start()
+    sends.append(copy)
+    window_arrival(1).wait_recv()
+    copy = window_copy(5, 1)
+    copy.start()
+    sends.append(copy)
+    copy = window_swap(1, core)
+    copy.start()
+    sends.append(copy)
     window_swap(4, 1 - core).wait_recv()
     slash_near()
-
     for half in range(2):
         for k in order:
             spread_one(half, k).wait_recv()
@@ -313,32 +326,31 @@
             copy.start()
             sends.append(copy)
     start_swap(0)
-    window_arrival(1).wait_recv()
-    copy = window_copy(5, 1)
+    window_arrival(3).wait_recv()
+    copy = window_swap(3, core)
     copy.start()
     sends.append(copy)
     end_swap(0)
     vertical_step(0)
-    for d in (1, 3, 2):
-        if d > 1:
-            window_arrival(d).wait_recv()
-        copy = window_swap(d, core)
-        copy.start()
-        sends.append(copy)
+    window_arrival(2).wait_recv()
+    copy = window_swap(2, core)
+    copy.start()
+    sends.append(copy)
+    window_arrival(5).wait_recv()
+    copy = window_swap(5, core)
+    copy.start()
+    sends.append(copy)
     arrive(1)
     arrive(3)
-    for d in (1, 2, 3):
-        window_swap(d, 1 - core).wait_recv()
+    window_swap(2, 1 - core).wait_recv()
+    window_swap(3, 1 - core).wait_recv()
     slash_middle()
     end_swap(1)
     vertical_step(1)
-    window_arrival(5).wait_recv()
-    copy = window_swap(5, core)
-    copy.start()
-    sends.append(copy)
-    arrive(2)
     end_swap(3)
     vertical_step(3)
+    arrive(2)
+    window_swap(1, 1 - core).wait_recv()
     window_swap(5, 1 - core).wait_recv()
     slash_far()
     end_swap(2)

time: 50.6 us -> 48.1 us (0.951)
  Pallas kernels: 48.8 us -> 46.3 us
    pallas_call x1, Pallas kernels: 48.8 us -> 46.3 us  [on_device(): pl.pallas_call(kernel, out_shape=jax.ShapeDtypeStruct((512, 256), BF16),...]
where the time goes in v4:
time: 48.1 us; the launch traced here: 48 us
  Pallas kernels  46.3 us (96%)
  local copies, waits for them, and re-layouts  1.67 us (3%)
    pallas_call x1, Pallas kernels, on_device(): pl.pallas_call(kernel, out_shape=jax.ShapeDtypeStruct((512, 256), BF16),...  46.3 us
    unnamed x1, local copies, waits for them, and re-layouts  1.67 us

profile of v4, /device:TPU:1, one launch (start us, length us, event | category | flops | bytes accessed | tf_op | source)
XLA Modules:
  0.0 48.0 jit_solution(7568468861624493605)
XLA Ops:
  0.0 46.3 %shard_map.64 = bf16[512,256]{1,0:T(8,128)(2,1)} custom-call(bf16[512,32,128]{2,1,0:T(8,128)(2,1)} %q_hbm.1, bf16[4096,256]{1,0:T(8,128)(2,1)} %bitcast.2, bf16[2048,256]{1,0:T(8,128)(2,1)} %bitcast.3, s32[8,64]{1,0:T(8,128)} %vertical_hbm.1, s32[32,32]{1,0:T(8,128)} %offsets_hbm.1, s32[1024]{0:T(1024)} %home_hbm.1), custom_call_target="tpu_custom_call" | custom-call | flops 7000000000 | bytes 6000000 | tf_op jit(solution)/shard_map/pallas_call | solution.py:371
  46.3 1.7 %copy.8 = bf16[512,256]{1,0:T(8,128)(2,1)} copy(bf16[512,256]{1,0:T(8,128)(2,1)} %shard_map.64) | data formatting | bytes 524288

commit v5 on v4

--- a/solution.py
+++ b/solution.py
@@ -229,7 +229,7 @@
             spread_two(half, k).wait_recv()
         start_swap(k)
 
-    def attend(b, keys, bias=None, diagonal=False, first=False):
+    def attend(b, keys, bias=None, diagonal=False, first=False, last=False):
         rows = pl.ds(b * 128, 128)
         n = keys.shape[0]
         scores = lax.dot_general(qb[b], keys[:, :128], (((1,), (1,)), ((), ())), preferred_element_type=F32)
@@ -253,8 +253,13 @@
             acc[rows, :] = add
         else:
             fade = jnp.exp2((old - new) * SCALE)
-            top[rows, :] = new
-            acc[rows, :] = acc[rows, :] * jnp.concatenate([fade, fade], 1) + add
+            total = acc[rows, :] * jnp.concatenate([fade, fade], 1) + add
+            if last:
+                result = (total[:, :128] / total[:, 128:]).astype(BF16)
+                out[pl.ds(b * 64, 64), :] = jnp.concatenate([result[:64], result[64:]], 1)
+            else:
+                top[rows, :] = new
+                acc[rows, :] = total
 
     def band_part(start, count, d):
         return band[:, pl.ds(start, count)] + jnp.where(c >= d, 0.0, MASKED)
@@ -279,9 +284,9 @@
             bias = [band_part(0, 512 - 128 * p, 5), band_part(2048 - 128 * p, 512, 1)]
             attend(b, keys, jnp.concatenate(bias, 1))
 
-    def vertical_step(k):
+    def vertical_step(k, last=False):
         for b in range(8):
-            attend(b, vert[pl.ds(k * 1024, 1024), :])
+            attend(b, vert[pl.ds(k * 1024, 1024), :], last=last)
 
     window_arrival(4).wait_recv()
     copy = window_copy(1, jnp.where(y + 1 < NY, 0, 4))
@@ -340,26 +345,21 @@
     copy = window_swap(5, core)
     copy.start()
     sends.append(copy)
-    arrive(1)
-    arrive(3)
     window_swap(2, 1 - core).wait_recv()
     window_swap(3, 1 - core).wait_recv()
     slash_middle()
-    end_swap(1)
-    vertical_step(1)
-    end_swap(3)
-    vertical_step(3)
-    arrive(2)
+    arrive(1)
+    arrive(3)
     window_swap(1, 1 - core).wait_recv()
     window_swap(5, 1 - core).wait_recv()
     slash_far()
+    end_swap(1)
+    vertical_step(1)
+    arrive(2)
+    end_swap(3)
+    vertical_step(3)
     end_swap(2)
-    vertical_step(2)
-
-    for b in range(8):
-        for h in range(2):
-            rows = pl.ds(b * 128 + h * 64, 64)
-            out[pl.ds(b * 64, 64), pl.ds(h * 128, 128)] = (acc[rows, :128] / acc[rows, 128:]).astype(BF16)
+    vertical_step(2, last=True)
 
     for copy in sends:
         copy.wait_send()

time: 48.1 us -> 47.3 us (0.983)
  Pallas kernels: 46.3 us -> 45.5 us
    pallas_call x1, Pallas kernels: 46.3 us -> 45.5 us  [on_device(): pl.pallas_call(kernel, out_shape=jax.ShapeDtypeStruct((512, 256), BF16),...]
where the time goes in v5:
time: 47.3 us; the launch traced here: 47.2 us
  Pallas kernels  45.5 us (96%)
  local copies, waits for them, and re-layouts  1.67 us (4%)
    pallas_call x1, Pallas kernels, on_device(): pl.pallas_call(kernel, out_shape=jax.ShapeDtypeStruct((512, 256), BF16),...  45.5 us
    unnamed x1, local copies, waits for them, and re-layouts  1.67 us

profile of v5, /device:TPU:1, one launch (start us, length us, event | category | flops | bytes accessed | tf_op | source)
XLA Modules:
  0.0 47.2 jit_solution(2599275656833565498)
XLA Ops:
  0.0 45.5 %shard_map.64 = bf16[512,256]{1,0:T(8,128)(2,1)} custom-call(bf16[512,32,128]{2,1,0:T(8,128)(2,1)} %q_hbm.1, bf16[4096,256]{1,0:T(8,128)(2,1)} %bitcast.2, bf16[2048,256]{1,0:T(8,128)(2,1)} %bitcast.3, s32[8,64]{1,0:T(8,128)} %vertical_hbm.1, s32[32,32]{1,0:T(8,128)} %offsets_hbm.1, s32[1024]{0:T(1024)} %home_hbm.1), custom_call_target="tpu_custom_call" | custom-call | flops 7000000000 | bytes 6000000 | tf_op jit(solution)/shard_map/pallas_call | solution.py:371
  45.5 1.7 %copy.8 = bf16[512,256]{1,0:T(8,128)(2,1)} copy(bf16[512,256]{1,0:T(8,128)(2,1)} %shard_map.64) | data formatting | bytes 524288

commit v6 on v5

--- a/solution.py
+++ b/solution.py
@@ -341,13 +341,13 @@
     copy = window_swap(2, core)
     copy.start()
     sends.append(copy)
-    window_arrival(5).wait_recv()
-    copy = window_swap(5, core)
-    copy.start()
-    sends.append(copy)
     window_swap(2, 1 - core).wait_recv()
     window_swap(3, 1 - core).wait_recv()
     slash_middle()
+    window_arrival(5).wait_recv()
+    copy = window_swap(5, core)
+    copy.start()
+    sends.append(copy)
     arrive(1)
     arrive(3)
     window_swap(1, 1 - core).wait_recv()

time: 47.3 us -> 48.1 us (1.017)
  Pallas kernels: 45.5 us -> 46.3 us
    pallas_call x1, Pallas kernels: 45.5 us -> 46.3 us  [on_device(): pl.pallas_call(kernel, out_shape=jax.ShapeDtypeStruct((512, 256), BF16),...]
where the time goes in v6:
time: 48.1 us; the launch traced here: 48 us
  Pallas kernels  46.3 us (96%)
  local copies, waits for them, and re-layouts  1.67 us (3%)
    pallas_call x1, Pallas kernels, on_device(): pl.pallas_call(kernel, out_shape=jax.ShapeDtypeStruct((512, 256), BF16),...  46.3 us
    unnamed x1, local copies, waits for them, and re-layouts  1.67 us

profile of v6, /device:TPU:1, one launch (start us, length us, event | category | flops | bytes accessed | tf_op | source)
XLA Modules:
  0.0 48.0 jit_solution(14107997077308733399)
XLA Ops:
  0.0 46.3 %shard_map.64 = bf16[512,256]{1,0:T(8,128)(2,1)} custom-call(bf16[512,32,128]{2,1,0:T(8,128)(2,1)} %q_hbm.1, bf16[4096,256]{1,0:T(8,128)(2,1)} %bitcast.2, bf16[2048,256]{1,0:T(8,128)(2,1)} %bitcast.3, s32[8,64]{1,0:T(8,128)} %vertical_hbm.1, s32[32,32]{1,0:T(8,128)} %offsets_hbm.1, s32[1024]{0:T(1024)} %home_hbm.1), custom_call_target="tpu_custom_call" | custom-call | flops 7000000000 | bytes 6000000 | tf_op jit(solution)/shard_map/pallas_call | solution.py:371
  46.3 1.7 %copy.8 = bf16[512,256]{1,0:T(8,128)(2,1)} copy(bf16[512,256]{1,0:T(8,128)(2,1)} %shard_map.64) | data formatting | bytes 524288
